TPU v7x, 32 devices: a whole 2x2x4 slice. The times are simulated.
32 devices in a mesh: frame: 16 (over z, y, core), pos: 2 (over x).
Axes of the slice: x: 2, y: 2, z: 4, core: 2. Of those that a mesh axis runs over, the one named last changes fastest.
Arguments:
- spatial_qkv: bfloat16 [2, 16, 384, 3, 1152], P(None, 'frame', 'pos'), may hold values from -9 to 9
- residual: bfloat16 [2, 16, 384, 1152], P(None, 'frame', 'pos'), may hold values from -0.59765625 to 0.59765625
- spatial_gate: float32 [2, 1152], replicated, may hold values from 0.5 to 2
- spatial_proj: bfloat16 [1152, 1152], replicated, may hold values from -0.1875 to 0.1875
- spatial_qgain: float32 [72], replicated, may hold values from 0.5 to 8
- spatial_kgain: float32 [72], replicated, may hold values from 0.5 to 8
- temporal_shift: float32 [2, 1152], replicated, may hold values from -3 to 3
- temporal_scale: float32 [2, 1152], replicated, may hold values from -0.5 to 0.5
- temporal_qkv: bfloat16 [1152, 3456], replicated, as said below
- temporal_qgain: float32 [72], replicated, may hold values from 0.6 to 6
- temporal_kgain: float32 [72], replicated, may hold values from 0.6 to 6
Outputs:
- temporal_out: bfloat16 [2, 16, 384, 1152], P(None, 'frame', 'pos')
Inputs may be any that keep to these rules, and one draw needn't show every extreme that they name: `temporal_qkv`: entries are of the size of a weight with fan-in 1152.
All inputs are finite; a program needn't handle non-finite values.
Results may differ from a plain program's by a relative error of at most 0.028.
The roundings to bfloat16 on the way count: a program that leaves them out, or rounds other values in their place, can miss the bound.
Values may be sent and summed in bfloat16 or wider, within the bound.
No kernel may reach another device: no remote copies, remote signals or barrier semaphores. Data moves between devices by JAX's collectives and lax.ppermute only.
A program may use at most 128 MiB of HBM per device.

v0:
```python
import math
import jax
import jax.numpy as jnp
from jax import lax
from jax.sharding import PartitionSpec as P

EPSILON = 1e-06


def head_norm(values, gain):
    widened = values.astype(jnp.float32)
    factor = lax.rsqrt(jnp.mean(widened * widened, axis=-1, keepdims=True) + EPSILON)
    return (widened * factor * gain).astype(jnp.bfloat16)


def softmax_weights(scores):
    row_top = jnp.max(scores, axis=-1, keepdims=True)
    expons = jnp.exp(scores - row_top)
    return (expons / jnp.sum(expons, axis=-1, keepdims=True)).astype(jnp.bfloat16)


def spatial_attend(element, query_gain, keys_gain):
    query_norm = head_norm(element[:, 0], query_gain)
    keys_norm = head_norm(element[:, 1], keys_gain)
    scores = jnp.einsum(
        "qhd,khd->hqk", query_norm, keys_norm, preferred_element_type=jnp.float32
    ) / math.sqrt(element.shape[-1])
    weights = softmax_weights(scores)
    return jnp.einsum(
        "hqk,khd->qhd", weights, element[:, 2], preferred_element_type=jnp.float32
    ).astype(jnp.bfloat16)


def per_device(
    spatial_qkv,
    residual,
    spatial_gate,
    spatial_proj,
    spatial_qgain,
    spatial_kgain,
    temporal_shift,
    temporal_scale,
    temporal_qkv,
    temporal_qgain,
    temporal_kgain,
):
    videos, frames_loc, pos_loc, triple, width = spatial_qkv.shape
    head_dim = spatial_qgain.shape[0]
    heads = width // head_dim
    pos_count = lax.axis_size("pos")
    frame_count = lax.axis_size("frame")
    heads_loc = heads // pos_count
    group_width = heads_loc * head_dim
    entries = videos * frames_loc
    all_pos = pos_count * pos_loc
    packed = spatial_qkv.reshape(entries, 1, pos_loc, 3, pos_count, group_width)
    by_heads = lax.all_to_all(packed, "pos", split_axis=4, concat_axis=1, tiled=True)
    by_heads = by_heads.reshape(entries, all_pos, 3, heads_loc, head_dim)
    attended = lax.map(
        lambda element: spatial_attend(element, spatial_qgain, spatial_kgain), by_heads
    )
    outgoing = attended.reshape(entries, pos_count, pos_loc, 1, group_width)
    returned = lax.all_to_all(outgoing, "pos", split_axis=1, concat_axis=3, tiled=True)
    mixed = jnp.dot(
        returned.reshape(entries * pos_loc, width), spatial_proj, preferred_element_type=jnp.float32
    )
    mixed = mixed.reshape(videos, frames_loc, pos_loc, width)
    updated = (residual.astype(jnp.float32) + spatial_gate[:, None, None, :] * mixed).astype(
        jnp.bfloat16
    )
    widened = updated.astype(jnp.float32)
    centred = widened - jnp.mean(widened, axis=-1, keepdims=True)
    spread = jnp.mean(centred * centred, axis=-1, keepdims=True)
    scaled = centred * lax.rsqrt(spread + EPSILON) * (1.0 + temporal_scale[:, None, None, :])
    normed = (scaled + temporal_shift[:, None, None, :]).astype(jnp.bfloat16)
    pos_group = pos_loc // frame_count
    frames_all = frames_loc * frame_count
    moved = lax.all_to_all(normed, "frame", split_axis=2, concat_axis=1, tiled=True)
    by_frames = jnp.dot(
        moved.reshape(videos * frames_all * pos_group, width),
        temporal_qkv,
        preferred_element_type=jnp.float32,
    )
    by_frames = by_frames.astype(jnp.bfloat16)
    arranged = by_frames.reshape(videos, frames_all, pos_group, 3, heads, head_dim)
    query_norm = head_norm(arranged[:, :, :, 0], temporal_qgain)
    keys_norm = head_norm(arranged[:, :, :, 1], temporal_kgain)
    scores = jnp.einsum(
        "bfphd,bgphd->bphfg", query_norm, keys_norm, preferred_element_type=jnp.float32
    ) / math.sqrt(head_dim)
    weights = softmax_weights(scores)
    result = jnp.einsum(
        "bphfg,bgphd->bfphd", weights, arranged[:, :, :, 2], preferred_element_type=jnp.float32
    )
    result = result.astype(jnp.bfloat16).reshape(videos, frames_all, pos_group, width)
    return lax.all_to_all(result, "frame", split_axis=1, concat_axis=2, tiled=True)


def solution(mesh):
    return jax.shard_map(
        per_device,
        mesh=mesh,
        in_specs=(
            P(None, "frame", "pos", None, None),
            P(None, "frame", "pos", None),
            P(),
            P(),
            P(),
            P(),
            P(),
            P(),
            P(),
            P(),
            P(),
        ),
        out_specs=P(None, "frame", "pos", None),
        check_vma=False,
    )
```

profile of v0, /device:TPU:1, one launch (start us, length us, event | category | flops | bytes accessed | tf_op | source)
XLA Modules:
  0.0 225.3 jit_solution(17201572388065575915)
XLA Ops:
  0.0 7.5 %reshape.113 = bf16[2,1,192,3,2,576]{5,4,2,3,0,1:T(2,128)(2,1)} reshape(bf16[2,1,192,3,1152]{4,2,3,1,0:T(8,128)(2,1)} %param.13) | data formatting | bytes 5308416 | tf_op jit(solution)/shard_map/reshape | solution.py:56
  7.5 3.9 %copy.63 = bf16[2,1,192,3,2,576]{5,2,3,1,0,4:T(8,128)(2,1)} copy(bf16[2,1,192,3,2,576]{5,4,2,3,0,1:T(2,128)(2,1)} %reshape.113) | data formatting | bytes 5308416 | tf_op jit(solution)/shard_map/reshape | solution.py:56
  11.4 5.1 %all-to-all-start = ((bf16[2,1,192,3,2,576]{5,2,3,1,0,4:T(8,128)(2,1)}), bf16[2,1,192,3,2,576]{5,2,3,1,0,4:T(8,128)(2,1)}, u32[]{:S(2)}, u32[]{:S(2)}) async-start(bf16[2,1,192,3,2,576]{5,2,3,1,0,4:T(8,128)(2,1)} %copy.63), calls=%async_computation | async-start | bytes 5898240 | tf_op jit(solution)/shard_map/all_to_all | solution.py:57
  16.5 34.4 %all-to-all-done = bf16[2,1,192,3,2,576]{5,2,3,1,0,4:T(8,128)(2,1)} async-done(((bf16[2,1,192,3,2,576]{5,2,3,1,0,4:T(8,128)(2,1)}), bf16[2,1,192,3,2,576]{5,2,3,1,0,4:T(8,128)(2,1)}, u32[]{:S(2)}, u32[]{:S(2)}) %all-to-all-start) | async-done | bytes 2654240 | tf_op jit(solution)/shard_map/all_to_all | solution.py:57
  50.9 9.1 %copy.64 = bf16[2,2,1,192,3,1,576]{3,1,6,4,0,5,2:T(2,128)(2,1)} copy(bf16[2,2,1,192,3,1,576]{6,3,4,0,1,5,2:T(8,128)(2,1)} %bitcast.10) | data formatting | bytes 5308416 | tf_op jit(solution)/shard_map/all_to_all | solution.py:57
  60.0 8.2 %reshape.114 = bf16[2,384,3,8,72]{1,4,3,2,0:T(8,128)(2,1)} reshape(bf16[2,2,1,192,3,1,576]{3,1,6,4,0,5,2:T(2,128)(2,1)} %copy.64) | data formatting | bytes 5308416 | tf_op jit(solution)/shard_map/reshape | solution.py:58
  68.2 23.9 %while.10 = (s32[]{:T(128)}, bf16[2,384,8,72]{1,3,2,0:T(8,128)(2,1)S(1)}, bf16[2,384,3,8,72]{1,4,3,2,0:T(8,128)(2,1)}, f32[72]{0:T(128)S(1)}, f32[72]{0:T(128)}, /*index=5*/s32[]{:T(128)}) while((s32[]{:T(128)}, bf16[2,384,8,72]{1,3,2,0:T(8,128)(2,1)S(1)}, bf16[2,384,3,8,72]{1,4,3,2,0:T(8,128)(2,1)}, f32[72]{0:T(128)S(1)}, f32[72]{0:T(128)}, ...), condition=%wide.region_5.6_spmd, body=%wide.region_0.5_spmd.sunk | while | flops 348961152 | bytes 20178308 | solution.py:59
  68.2 1.5 dynamic-slice_bitcast_fusion.2
  69.6 1.1 copy-done.1
  71.6 5.5 %fusion.78 = (f32[8,384]{1,0:T(8,128)}, f32[8,384,384]{1,2,0:T(8,128)}) fusion(f32[72]{0:T(128)} %get-tuple-element.117, f32[384,8]{0,1:T(8,128)S(1)} %get-tuple-element.97, bf16[384,3,8,72]{0,3,2,1:T(8,128)(2,1)} %copy-done.1, f32[72]{0:T(128)S(1)} %get-tuple-element.116, f32[384,8]{0,1:T(8,128)} %get-tuple-element.98), kind=kOutput, calls=%fused_computation.71.clone.1 | convolution fusion | flops 175178112 | bytes 5640992 | tf_op jit(solution)/shard_map/while/body/eval_jaxpr/sub | solution.py:18
  77.1 3.0 %fusion.79 = bf16[2,384,8,72]{1,3,2,0:T(8,128)(2,1)S(1)} fusion(bf16[2,384,8,72]{1,3,2,0:T(8,128)(2,1)S(1)} %get-tuple-element.108, s32[]{:T(128)} %get-tuple-element.107, f32[8,384,384]{1,2,0:T(8,128)} %get-tuple-element.99, f32[8,384]{1,0:T(8,128)} %get-tuple-element.100, bf16[384,3,8,72]{0,3,2,1:T(8,128)(2,1)} %copy-done.1), kind=kOutput, calls=%fused_computation.10.clone.1 | convolution fusion | flops 172449792 | bytes 5616128 | tf_op jit(solution)/shard_map/while/body/eval_jaxpr/hqk,khd->qhd/dot_general | solution.py:29
  80.1 1.5 dynamic-slice_bitcast_fusion.2
  83.6 5.5 %fusion.78 = (f32[8,384]{1,0:T(8,128)}, f32[8,384,384]{1,2,0:T(8,128)}) fusion(f32[72]{0:T(128)} %get-tuple-element.117, f32[384,8]{0,1:T(8,128)S(1)} %get-tuple-element.97, bf16[384,3,8,72]{0,3,2,1:T(8,128)(2,1)} %copy-done.1, f32[72]{0:T(128)S(1)} %get-tuple-element.116, f32[384,8]{0,1:T(8,128)} %get-tuple-element.98), kind=kOutput, calls=%fused_computation.71.clone.1 | convolution fusion | flops 175178112 | bytes 5640992 | tf_op jit(solution)/shard_map/while/body/eval_jaxpr/sub | solution.py:18
  89.1 3.0 %fusion.79 = bf16[2,384,8,72]{1,3,2,0:T(8,128)(2,1)S(1)} fusion(bf16[2,384,8,72]{1,3,2,0:T(8,128)(2,1)S(1)} %get-tuple-element.108, s32[]{:T(128)} %get-tuple-element.107, f32[8,384,384]{1,2,0:T(8,128)} %get-tuple-element.99, f32[8,384]{1,0:T(8,128)} %get-tuple-element.100, bf16[384,3,8,72]{0,3,2,1:T(8,128)(2,1)} %copy-done.1), kind=kOutput, calls=%fused_computation.10.clone.1 | convolution fusion | flops 172449792 | bytes 5616128 | tf_op jit(solution)/shard_map/while/body/eval_jaxpr/hqk,khd->qhd/dot_general | solution.py:29
  92.1 1.6 reshape.115
  93.7 3.7 %copy.65 = bf16[2,2,192,1,576]{4,2,3,0,1:T(8,128)(2,1)} copy(bf16[2,2,192,1,576]{2,1,4,0,3:T(2,128)(2,1)} %reshape.115) | data formatting | bytes 1769472 | tf_op jit(solution)/shard_map/reshape | solution.py:62
  97.5 4.6 %all-to-all-start.1 = ((bf16[2,2,192,1,576]{4,2,3,0,1:T(8,128)(2,1)}), bf16[2,2,192,1,576]{4,2,3,0,1:T(8,128)(2,1)}, u32[]{:S(2)}, u32[]{:S(2)}) async-start(bf16[2,2,192,1,576]{4,2,3,0,1:T(8,128)(2,1)} %copy.65), calls=%async_computation.1 | async-start | bytes 1966080 | tf_op jit(solution)/shard_map/all_to_all | solution.py:63
  102.0 11.6 %all-to-all-done.1 = bf16[2,2,192,1,576]{4,2,3,0,1:T(8,128)(2,1)} async-done(((bf16[2,2,192,1,576]{4,2,3,0,1:T(8,128)(2,1)}), bf16[2,2,192,1,576]{4,2,3,0,1:T(8,128)(2,1)}, u32[]{:S(2)}, u32[]{:S(2)}) %all-to-all-start.1) | async-done | bytes 884768 | tf_op jit(solution)/shard_map/all_to_all | solution.py:63
  113.6 3.2 %copy.66 = bf16[2,1,192,2,1,576]{5,3,2,0,4,1:T(2,128)(2,1)} copy(bf16[2,1,192,2,1,576]{5,2,0,3,4,1:T(8,128)(2,1)} %bitcast.12) | data formatting | bytes 1769472 | tf_op jit(solution)/shard_map/all_to_all | solution.py:63
  116.8 2.4 %dot_general.20 = bf16[2,192,1152]{2,1,0:T(8,128)(2,1)S(1)} reshape(bf16[2,1,192,2,1,576]{5,3,2,0,4,1:T(2,128)(2,1)} %copy.66) | data formatting | bytes 1769472 | tf_op jit(solution)/shard_map/dot_general | solution.py:64
  119.3 2.9 %fusion.65 = (f32[2,192]{1,0:T(2,128)S(1)}, f32[2,1,192,1152]{3,2,0,1:T(8,128)S(1)}) fusion(bf16[2,192,1152]{2,1,0:T(8,128)(2,1)S(1)} %dot_general.20, bf16[1152,1152]{1,0:T(8,128)(2,1)S(1)} %copy-done, f32[2,1152]{1,0:T(2,128)} %param.15, bf16[2,1,192,1152]{3,2,1,0:T(8,128)(2,1)} %param.14), kind=kOutput, calls=%fused_computation.73 | convolution fusion | flops 1021869696 | bytes 6203904 | tf_op jit(solution)/shard_map/dot_general | solution.py:64
  123.8 30.0 %all_to_all.51 = bf16[2,1,192,1152]{3,0,1,2:T(2,128)(2,1)S(1)} all-to-all(bf16[2,1,192,1152]{3,0,1,2:T(2,128)(2,1)S(1)} %copy.67), channel_id=1, replica_groups=mesh['frame'=16,'pos'=2] {'frame'}, dimensions={2} | all-to-all | bytes 1769472 | tf_op jit(solution)/shard_map/all_to_all | solution.py:78
  154.0 5.0 %convolution_convert_fusion = bf16[384,3456]{1,0:T(8,128)(2,1)} fusion(bf16[384,1152]{1,0:T(8,128)(2,1)S(1)} %bitcast.121, bf16[1152,3456]{1,0:T(8,128)(2,1)S(1)} %bitcast.123), kind=kOutput, calls=%fused_computation.30 | convolution fusion | flops 3058974720 | bytes 11501568 | tf_op jit(solution)/shard_map/dot_general | solution.py:79
  159.0 10.7 %reshape.117 = bf16[2,16,12,3,16,72]{5,4,3,2,1,0:T(8,128)(2,1)} reshape(bf16[384,3456]{1,0:T(8,128)(2,1)} %convolution_convert_fusion) | data formatting | bytes 5308416 | tf_op jit(solution)/shard_map/reshape | solution.py:85
  169.7 3.3 %fusion.64 = (bf16[2,16,12,1,16,72]{5,4,3,2,1,0:T(8,128)(2,1)S(1)}, bf16[2,16,12,1,16,72]{5,4,3,2,1,0:T(8,128)(2,1)S(1)}, bf16[2,16,12,1,16,72]{5,4,3,2,1,0:T(8,128)(2,1)S(1)}) fusion(bf16[2,16,12,3,16,72]{5,4,3,2,1,0:T(8,128)(2,1)} %reshape.117), kind=kLoop, calls=%fused_computation.72 | loop fusion | bytes 5308416 | tf_op jit(solution)/shard_map/slice | solution.py:93
  173.0 2.2 fusion.30
  175.3 2.4 %fusion.44 = f32[2,12,16,16,16]{3,4,2,1,0:T(8,128)S(1)} fusion(f32[72]{0:T(128)S(1)} %copy-done.5, f32[2,16,12,16]{1,3,2,0:T(8,128)S(1)} %add_rsqrt_fusion.2, f32[72]{0:T(128)S(1)} %copy-done.6, f32[2,16,12,16]{1,3,2,0:T(8,128)S(1)} %add_rsqrt_fusion.3, bf16[2,16,12,1,16,72]{5,4,3,2,1,0:T(8,128)(2,1)S(1)} %get-tuple-element.50, ...), kind=kOutput, calls=%fused_computation.54 | convolution fusion | flops 17694720 | bytes 2212416 | tf_op jit(solution)/shard_map/bfphd,bgphd->bphfg/dot_general | solution.py:88
  177.7 13.3 %fusion.66 = (f32[2,12,16,16]{3,2,1,0:T(8,128)S(1)}, f32[2,12,16,16,16]{3,4,2,1,0:T(8,128)S(1)}) fusion(f32[2,12,16,16,16]{3,4,2,1,0:T(8,128)S(1)} %fusion.44), kind=kOutput, calls=%fused_computation.74 | output fusion | flops 393231 | bytes 811008 | tf_op jit(solution)/shard_map/sub | solution.py:18
  191.0 1.2 fusion.53
  192.3 1.6 copy.78
  193.8 4.3 %reshape.124 = bf16[2,16,12,1152]{3,0,2,1:T(2,128)(2,1)S(1)} reshape(bf16[2,16,12,16,72]{4,3,0,2,1:T(8,128)(2,1)} %copy.78) | data formatting | bytes 1769472 | tf_op jit(solution)/shard_map/reshape | solution.py:95
  198.2 26.1 %all_to_all.52 = bf16[2,16,12,1152]{3,0,2,1:T(2,128)(2,1)S(1)} all-to-all(bf16[2,16,12,1152]{3,0,2,1:T(2,128)(2,1)S(1)} %reshape.124), channel_id=1, replica_groups=mesh['frame'=16,'pos'=2] {'frame'}, dimensions={1} | all-to-all | bytes 1769472 | tf_op jit(solution)/shard_map/all_to_all | solution.py:96
  (35 shorter events, 5.6 us)
Async XLA Ops:
  0.0 119.2 %copy-start = (bf16[1152,1152]{1,0:T(8,128)(2,1)S(1)}, bf16[1152,1152]{1,0:T(8,128)(2,1)}, u32[]{:S(2)}) copy-start(bf16[1152,1152]{1,0:T(8,128)(2,1)} %param.16) | copy-start | bytes 7962628
  11.4 39.5 %all-to-all-start = ((bf16[2,1,192,3,2,576]{5,2,3,1,0,4:T(8,128)(2,1)}), bf16[2,1,192,3,2,576]{5,2,3,1,0,4:T(8,128)(2,1)}, u32[]{:S(2)}, u32[]{:S(2)}) async-start(bf16[2,1,192,3,2,576]{5,2,3,1,0,4:T(8,128)(2,1)} %copy.63), calls=%async_computation | async-start | bytes 5898240 | tf_op jit(solution)/shard_map/all_to_all | solution.py:57
  60.0 8.2 %copy-start.4 = (f32[72]{0:T(128)S(1)}, f32[72]{0:T(128)}, u32[]{:S(2)}) copy-start(f32[72]{0:T(128)} %param.17) | copy-start | bytes 868
  69.6 1.1 copy-start.1
  81.6 1.1 copy-start.1
  93.7 8.3 %copy-start.3 = (f32[2,1152]{1,0:T(2,128)S(1)}, f32[2,1152]{1,0:T(2,128)}, u32[]{:S(2)}) copy-start(f32[2,1152]{1,0:T(2,128)} %param.20) | copy-start | bytes 27652
  97.5 16.2 %all-to-all-start.1 = ((bf16[2,2,192,1,576]{4,2,3,0,1:T(8,128)(2,1)}), bf16[2,2,192,1,576]{4,2,3,0,1:T(8,128)(2,1)}, u32[]{:S(2)}, u32[]{:S(2)}) async-start(bf16[2,2,192,1,576]{4,2,3,0,1:T(8,128)(2,1)} %copy.65), calls=%async_computation.1 | async-start | bytes 1966080 | tf_op jit(solution)/shard_map/all_to_all | solution.py:63
  119.3 3.3 %copy-start.2 = (f32[2,1152]{1,0:T(2,128)S(1)}, f32[2,1152]{1,0:T(2,128)}, u32[]{:S(2)}) copy-start(f32[2,1152]{1,0:T(2,128)} %param.19) | copy-start | bytes 27652
  119.3 34.7 %slice-start = ((s8[7962624]{0:T(1024)(128)(4,1)}), s8[4194304]{0:T(1024)(128)(4,1)S(1)}, s32[]{:S(2)}) async-start(s8[7962624]{0:T(1024)(128)(4,1)} %bitcast.122), calls=%async_computation.4 | async-start | bytes 8388608
  122.2 31.8 %slice-start.1 = ((s8[7962624]{0:T(1024)(128)(4,1)}), s8[3768320]{0:T(1024)(128)(4,1)S(1)}, s32[]{:S(2)}) async-start(s8[7962624]{0:T(1024)(128)(4,1)} %bitcast.122), calls=%async_computation.5 | async-start | bytes 7536640
  173.0 2.3 %copy-start.5 = (f32[72]{0:T(128)S(1)}, f32[72]{0:T(128)}, u32[]{:S(2)}) copy-start(f32[72]{0:T(128)} %param.23) | copy-start | bytes 868
  173.0 2.3 %copy-start.6 = (f32[72]{0:T(128)S(1)}, f32[72]{0:T(128)}, u32[]{:S(2)}) copy-start(f32[72]{0:T(128)} %param.22) | copy-start | bytes 868
where the time goes:
time: 226 us; the launch traced here: 225 us
  local copies, waits for them, and re-layouts  66.7 us (30%)
  blocking collectives  56.2 us (25%)
  waiting for transfers between devices  45.9 us (20%)
  matrix products  28.6 us (13%)
  other arithmetic  18 us (8%)
  starting transfers between devices  9.67 us (4%)
    all_to_all x1, waiting for transfers between devices, per_device(): lax.all_to_all(packed, 'pos', split_axis=4, concat_axis=1, tiled=True)  34.4 us
    all_to_all x1, blocking collectives, per_device(): lax.all_to_all(normed, 'frame', split_axis=2, concat_axis=1, tiled=True)  30 us
    all_to_all x1, blocking collectives, per_device(): lax.all_to_all(result, 'frame', split_axis=1, concat_axis=2, tiled=True)  26.1 us
    sub x1, other arithmetic, softmax_weights(): expons = jnp.exp(scores - row_top)  13.3 us
    all_to_all x1, waiting for transfers between devices, per_device(): lax.all_to_all(outgoing, 'pos', split_axis=1, concat_axis=3, tiled=True)  11.6 us
    reshape x2, local copies, waits for them, and re-layouts, per_device(): packed = spatial_qkv.reshape(entries, 1, pos_loc, 3, pos_count, group_width)  11.4 us
    sub x2, matrix products, softmax_weights(): expons = jnp.exp(scores - row_top)  11.1 us
    reshape x1, local copies, waits for them, and re-layouts, per_device(): by_frames.reshape(videos, frames_all, pos_group, 3, heads, head_dim)  10.7 us
  transfers between devices with their start and end apart: 2, of which 2 were waited for; matrix products, arithmetic and copies ran while one was open for 0% of the time, Pallas kernels for 0%

commit v1 on v0

--- a/solution.py
+++ b/solution.py
@@ -60,7 +60,10 @@
         lambda element: spatial_attend(element, spatial_qgain, spatial_kgain), by_heads
     )
     outgoing = attended.reshape(entries, pos_count, pos_loc, 1, group_width)
-    returned = lax.all_to_all(outgoing, "pos", split_axis=1, concat_axis=3, tiled=True)
+    returned = jnp.concatenate(
+        lax.all_to_all(jnp.stack(jnp.split(outgoing, lax.axis_size("pos"), axis=1)), "pos", 0, 0),
+        axis=3,
+    )
     mixed = jnp.dot(
         returned.reshape(entries * pos_loc, width), spatial_proj, preferred_element_type=jnp.float32
     )

time: 226 us -> 236 us (1.044)
  local copies, waits for them, and re-layouts: 66.7 us -> 74.3 us
    split x0 -> x3, local copies, waits for them, and re-layouts: none -> 11.4 us  [per_device(): jnp.split(outgoing, lax.axis_size('pos'), axis=1)]
    reshape x2 -> x1, local copies, waits for them, and re-layouts: 5.36 us -> 1.61 us  [per_device(): outgoing = attended.reshape(entries, pos_count, pos_loc, 1, group_width)]
    all_to_all x1 -> x0, local copies, waits for them, and re-layouts: 3.2 us -> none  [per_device(): lax.all_to_all(outgoing, 'pos', split_axis=1, concat_axis=3, tiled=True)]
    reshape x0 -> x1, local copies, waits for them, and re-layouts: none -> 3.2 us  [per_device(): jnp.concatenate(lax.all_to_all(jnp.stack(jnp.split(outgoing, lax.axis_siz...]
where the time goes in v1:
time: 236 us; the launch traced here: 235 us
  local copies, waits for them, and re-layouts  74.3 us (31%)
  blocking collectives  56.2 us (24%)
  waiting for transfers between devices  45.9 us (19%)
  matrix products  28.6 us (12%)
  other arithmetic  20.1 us (9%)
  starting transfers between devices  9.67 us (4%)
    all_to_all x1, waiting for transfers between devices, per_device(): lax.all_to_all(packed, 'pos', split_axis=4, concat_axis=1, tiled=True)  34.4 us
    all_to_all x1, blocking collectives, per_device(): lax.all_to_all(normed, 'frame', split_axis=2, concat_axis=1, tiled=True)  30 us
    all_to_all x1, blocking collectives, per_device(): lax.all_to_all(result, 'frame', split_axis=1, concat_axis=2, tiled=True)  26.1 us
    sub x1, other arithmetic, softmax_weights(): expons = jnp.exp(scores - row_top)  13.3 us
    all_to_all x1, waiting for transfers between devices, per_device(): lax.all_to_all(jnp.stack(jnp.split(outgoing, lax.axis_size('pos'), axis=1...  11.6 us
    reshape x2, local copies, waits for them, and re-layouts, per_device(): packed = spatial_qkv.reshape(entries, 1, pos_loc, 3, pos_count, group_width)  11.4 us
    split x3, local copies, waits for them, and re-layouts, per_device(): jnp.split(outgoing, lax.axis_size('pos'), axis=1)  11.4 us
    sub x2, matrix products, softmax_weights(): expons = jnp.exp(scores - row_top)  11.1 us
  transfers between devices with their start and end apart: 2, of which 2 were waited for; matrix products, arithmetic and copies ran while one was open for 0% of the time, Pallas kernels for 0%

profile of v1, /device:TPU:1, one launch (start us, length us, event | category | flops | bytes accessed | tf_op | source)
XLA Modules:
  0.0 235.1 jit_solution(16884090150981498797)
XLA Ops:
  0.0 7.5 %reshape.114 = bf16[2,1,192,3,2,576]{5,4,2,3,0,1:T(2,128)(2,1)} reshape(bf16[2,1,192,3,1152]{4,2,3,1,0:T(8,128)(2,1)} %param.13) | data formatting | bytes 5308416 | tf_op jit(solution)/shard_map/reshape | solution.py:56
  7.5 3.9 %copy.68 = bf16[2,1,192,3,2,576]{5,2,3,1,0,4:T(8,128)(2,1)} copy(bf16[2,1,192,3,2,576]{5,4,2,3,0,1:T(2,128)(2,1)} %reshape.114) | data formatting | bytes 5308416 | tf_op jit(solution)/shard_map/reshape | solution.py:56
  11.4 5.1 %all-to-all-start = ((bf16[2,1,192,3,2,576]{5,2,3,1,0,4:T(8,128)(2,1)}), bf16[2,1,192,3,2,576]{5,2,3,1,0,4:T(8,128)(2,1)}, u32[]{:S(2)}, u32[]{:S(2)}) async-start(bf16[2,1,192,3,2,576]{5,2,3,1,0,4:T(8,128)(2,1)} %copy.68), calls=%async_computation | async-start | bytes 5898240 | tf_op jit(solution)/shard_map/all_to_all | solution.py:57
  16.5 34.4 %all-to-all-done = bf16[2,1,192,3,2,576]{5,2,3,1,0,4:T(8,128)(2,1)} async-done(((bf16[2,1,192,3,2,576]{5,2,3,1,0,4:T(8,128)(2,1)}), bf16[2,1,192,3,2,576]{5,2,3,1,0,4:T(8,128)(2,1)}, u32[]{:S(2)}, u32[]{:S(2)}) %all-to-all-start) | async-done | bytes 2654240 | tf_op jit(solution)/shard_map/all_to_all | solution.py:57
  50.9 9.1 %copy.69 = bf16[2,2,1,192,3,1,576]{3,1,6,4,0,5,2:T(2,128)(2,1)} copy(bf16[2,2,1,192,3,1,576]{6,3,4,0,1,5,2:T(8,128)(2,1)} %bitcast.10) | data formatting | bytes 5308416 | tf_op jit(solution)/shard_map/all_to_all | solution.py:57
  60.0 8.2 %reshape.115 = bf16[2,384,3,8,72]{1,4,3,2,0:T(8,128)(2,1)} reshape(bf16[2,2,1,192,3,1,576]{3,1,6,4,0,5,2:T(2,128)(2,1)} %copy.69) | data formatting | bytes 5308416 | tf_op jit(solution)/shard_map/reshape | solution.py:58
  68.2 23.9 %while.10 = (s32[]{:T(128)}, bf16[2,384,8,72]{1,3,2,0:T(8,128)(2,1)S(1)}, bf16[2,384,3,8,72]{1,4,3,2,0:T(8,128)(2,1)}, f32[72]{0:T(128)S(1)}, f32[72]{0:T(128)}, /*index=5*/s32[]{:T(128)}) while((s32[]{:T(128)}, bf16[2,384,8,72]{1,3,2,0:T(8,128)(2,1)S(1)}, bf16[2,384,3,8,72]{1,4,3,2,0:T(8,128)(2,1)}, f32[72]{0:T(128)S(1)}, f32[72]{0:T(128)}, ...), condition=%wide.region_5.6_spmd, body=%wide.region_0.5_spmd.sunk | while | flops 348961152 | bytes 20178308 | solution.py:59
  71.6 5.5 %fusion.79 = (f32[8,384]{1,0:T(8,128)}, f32[8,384,384]{1,2,0:T(8,128)}) fusion(f32[72]{0:T(128)} %get-tuple-element.119, f32[384,8]{0,1:T(8,128)S(1)} %get-tuple-element.99, bf16[384,3,8,72]{0,3,2,1:T(8,128)(2,1)} %copy-done.1, f32[72]{0:T(128)S(1)} %get-tuple-element.118, f32[384,8]{0,1:T(8,128)} %get-tuple-element.100), kind=kOutput, calls=%fused_computation.72.clone.1 | convolution fusion | flops 175178112 | bytes 5640992 | tf_op jit(solution)/shard_map/while/body/eval_jaxpr/sub | solution.py:18
  77.1 3.0 %fusion.80 = bf16[2,384,8,72]{1,3,2,0:T(8,128)(2,1)S(1)} fusion(bf16[2,384,8,72]{1,3,2,0:T(8,128)(2,1)S(1)} %get-tuple-element.110, s32[]{:T(128)} %get-tuple-element.109, f32[8,384,384]{1,2,0:T(8,128)} %get-tuple-element.101, f32[8,384]{1,0:T(8,128)} %get-tuple-element.102, bf16[384,3,8,72]{0,3,2,1:T(8,128)(2,1)} %copy-done.1), kind=kOutput, calls=%fused_computation.10.clone.1 | convolution fusion | flops 172449792 | bytes 5616128 | tf_op jit(solution)/shard_map/while/body/eval_jaxpr/hqk,khd->qhd/dot_general | solution.py:29
  80.1 1.5 dynamic-slice_bitcast_fusion.2
  83.6 5.5 %fusion.79 = (f32[8,384]{1,0:T(8,128)}, f32[8,384,384]{1,2,0:T(8,128)}) fusion(f32[72]{0:T(128)} %get-tuple-element.119, f32[384,8]{0,1:T(8,128)S(1)} %get-tuple-element.99, bf16[384,3,8,72]{0,3,2,1:T(8,128)(2,1)} %copy-done.1, f32[72]{0:T(128)S(1)} %get-tuple-element.118, f32[384,8]{0,1:T(8,128)} %get-tuple-element.100), kind=kOutput, calls=%fused_computation.72.clone.1 | convolution fusion | flops 175178112 | bytes 5640992 | tf_op jit(solution)/shard_map/while/body/eval_jaxpr/sub | solution.py:18
  89.1 3.0 %fusion.80 = bf16[2,384,8,72]{1,3,2,0:T(8,128)(2,1)S(1)} fusion(bf16[2,384,8,72]{1,3,2,0:T(8,128)(2,1)S(1)} %get-tuple-element.110, s32[]{:T(128)} %get-tuple-element.109, f32[8,384,384]{1,2,0:T(8,128)} %get-tuple-element.101, f32[8,384]{1,0:T(8,128)} %get-tuple-element.102, bf16[384,3,8,72]{0,3,2,1:T(8,128)(2,1)} %copy-done.1), kind=kOutput, calls=%fused_computation.10.clone.1 | convolution fusion | flops 172449792 | bytes 5616128 | tf_op jit(solution)/shard_map/while/body/eval_jaxpr/hqk,khd->qhd/dot_general | solution.py:29
  92.1 1.6 reshape.116
  93.7 5.1 %fusion.65 = (bf16[2,1,192,1,576]{2,1,4,0,3:T(2,128)(2,1)}, bf16[2,1,192,1,576]{2,1,4,0,3:T(2,128)(2,1)}) fusion(bf16[2,2,192,1,576]{2,1,4,0,3:T(2,128)(2,1)} %reshape.116), kind=kLoop, calls=%fused_computation.74 | loop fusion | bytes 1769472 | tf_op jit(solution)/shard_map/split | solution.py:64
  98.8 2.7 %copy.70 = bf16[2,1,192,1,576]{4,2,0,3,1:T(8,128)(2,1)S(1)} copy(bf16[2,1,192,1,576]{2,1,4,0,3:T(2,128)(2,1)} %get-tuple-element.52) | data formatting | bytes 884736 | tf_op jit(solution)/shard_map/split | solution.py:64
  101.5 3.6 %copy.71 = bf16[2,1,192,1,576]{4,2,0,3,1:T(8,128)(2,1)} copy(bf16[2,1,192,1,576]{2,1,4,0,3:T(2,128)(2,1)} %get-tuple-element.53) | data formatting | bytes 884736 | tf_op jit(solution)/shard_map/split | solution.py:64
  105.1 2.2 pad_maximum_fusion
  107.2 4.6 %all-to-all-start.1 = ((bf16[2,2,1,192,1,576]{5,3,1,4,2,0:T(8,128)(2,1)}), bf16[2,2,1,192,1,576]{5,3,1,4,2,0:T(8,128)(2,1)}, u32[]{:S(2)}, u32[]{:S(2)}) async-start(bf16[2,2,1,192,1,576]{5,3,1,4,2,0:T(8,128)(2,1)} %pad_maximum_fusion), calls=%async_computation.1 | async-start | bytes 1966080 | tf_op jit(solution)/shard_map/all_to_all | solution.py:64
  111.8 11.6 %all-to-all-done.1 = bf16[2,2,1,192,1,576]{5,3,1,4,2,0:T(8,128)(2,1)} async-done(((bf16[2,2,1,192,1,576]{5,3,1,4,2,0:T(8,128)(2,1)}), bf16[2,2,1,192,1,576]{5,3,1,4,2,0:T(8,128)(2,1)}, u32[]{:S(2)}, u32[]{:S(2)}) %all-to-all-start.1) | async-done | bytes 884768 | tf_op jit(solution)/shard_map/all_to_all | solution.py:64
  123.4 3.2 %copy.72 = bf16[2,1,192,2,1,576]{5,3,2,0,4,1:T(2,128)(2,1)} copy(bf16[2,1,192,2,1,576]{5,2,0,4,1,3:T(8,128)(2,1)} %bitcast.13) | data formatting | bytes 1769472 | tf_op jit(solution)/shard_map/reshape | solution.py:63
  126.6 2.4 %dot_general.20 = bf16[2,192,1152]{2,1,0:T(8,128)(2,1)S(1)} reshape(bf16[2,1,192,2,1,576]{5,3,2,0,4,1:T(2,128)(2,1)} %copy.72) | data formatting | bytes 1769472 | tf_op jit(solution)/shard_map/dot_general | solution.py:67
  129.1 2.9 %fusion.66 = (f32[2,192]{1,0:T(2,128)S(1)}, f32[2,1,192,1152]{3,2,0,1:T(8,128)S(1)}) fusion(bf16[2,192,1152]{2,1,0:T(8,128)(2,1)S(1)} %dot_general.20, bf16[1152,1152]{1,0:T(8,128)(2,1)S(1)} %copy-done, f32[2,1152]{1,0:T(2,128)} %param.15, bf16[2,1,192,1152]{3,2,1,0:T(8,128)(2,1)} %param.14), kind=kOutput, calls=%fused_computation.75 | convolution fusion | flops 1021869696 | bytes 6203904 | tf_op jit(solution)/shard_map/dot_general | solution.py:67
  133.6 30.0 %all_to_all.41 = bf16[2,1,192,1152]{3,0,1,2:T(2,128)(2,1)S(1)} all-to-all(bf16[2,1,192,1152]{3,0,1,2:T(2,128)(2,1)S(1)} %copy.73), channel_id=1, replica_groups=mesh['frame'=16,'pos'=2] {'frame'}, dimensions={2} | all-to-all | bytes 1769472 | tf_op jit(solution)/shard_map/all_to_all | solution.py:81
  163.8 5.0 %convolution_convert_fusion = bf16[384,3456]{1,0:T(8,128)(2,1)} fusion(bf16[384,1152]{1,0:T(8,128)(2,1)S(1)} %bitcast.123, bf16[1152,3456]{1,0:T(8,128)(2,1)S(1)} %bitcast.125), kind=kOutput, calls=%fused_computation.30 | convolution fusion | flops 3058974720 | bytes 11501568 | tf_op jit(solution)/shard_map/dot_general | solution.py:82
  168.8 10.7 %reshape.119 = bf16[2,16,12,3,16,72]{5,4,3,2,1,0:T(8,128)(2,1)} reshape(bf16[384,3456]{1,0:T(8,128)(2,1)} %convolution_convert_fusion) | data formatting | bytes 5308416 | tf_op jit(solution)/shard_map/reshape | solution.py:88
  179.5 3.3 %fusion.64 = (bf16[2,16,12,1,16,72]{5,4,3,2,1,0:T(8,128)(2,1)S(1)}, bf16[2,16,12,1,16,72]{5,4,3,2,1,0:T(8,128)(2,1)S(1)}, bf16[2,16,12,1,16,72]{5,4,3,2,1,0:T(8,128)(2,1)S(1)}) fusion(bf16[2,16,12,3,16,72]{5,4,3,2,1,0:T(8,128)(2,1)} %reshape.119), kind=kLoop, calls=%fused_computation.73 | loop fusion | bytes 5308416 | tf_op jit(solution)/shard_map/slice | solution.py:96
  182.8 2.2 fusion.30
  185.1 2.4 %fusion.44 = f32[2,12,16,16,16]{3,4,2,1,0:T(8,128)S(1)} fusion(f32[72]{0:T(128)S(1)} %copy-done.5, f32[2,16,12,16]{1,3,2,0:T(8,128)S(1)} %add_rsqrt_fusion.2, f32[72]{0:T(128)S(1)} %copy-done.6, f32[2,16,12,16]{1,3,2,0:T(8,128)S(1)} %add_rsqrt_fusion.3, bf16[2,16,12,1,16,72]{5,4,3,2,1,0:T(8,128)(2,1)S(1)} %get-tuple-element.50, ...), kind=kOutput, calls=%fused_computation.54 | convolution fusion | flops 17694720 | bytes 2212416 | tf_op jit(solution)/shard_map/bfphd,bgphd->bphfg/dot_general | solution.py:91
  187.5 13.3 %fusion.67 = (f32[2,12,16,16]{3,2,1,0:T(8,128)S(1)}, f32[2,12,16,16,16]{3,4,2,1,0:T(8,128)S(1)}) fusion(f32[2,12,16,16,16]{3,4,2,1,0:T(8,128)S(1)} %fusion.44), kind=kOutput, calls=%fused_computation.76 | output fusion | flops 393231 | bytes 811008 | tf_op jit(solution)/shard_map/sub | solution.py:18
  202.0 1.6 copy.84
  203.6 4.3 %reshape.126 = bf16[2,16,12,1152]{3,0,2,1:T(2,128)(2,1)S(1)} reshape(bf16[2,16,12,16,72]{4,3,0,2,1:T(8,128)(2,1)} %copy.84) | data formatting | bytes 1769472 | tf_op jit(solution)/shard_map/reshape | solution.py:98
  208.0 26.1 %all_to_all.42 = bf16[2,16,12,1152]{3,0,2,1:T(2,128)(2,1)S(1)} all-to-all(bf16[2,16,12,1152]{3,0,2,1:T(2,128)(2,1)S(1)} %reshape.126), channel_id=1, replica_groups=mesh['frame'=16,'pos'=2] {'frame'}, dimensions={1} | all-to-all | bytes 1769472 | tf_op jit(solution)/shard_map/all_to_all | solution.py:99
  (38 shorter events, 9.4 us)
Async XLA Ops:
  0.0 129.0 %copy-start = (bf16[1152,1152]{1,0:T(8,128)(2,1)S(1)}, bf16[1152,1152]{1,0:T(8,128)(2,1)}, u32[]{:S(2)}) copy-start(bf16[1152,1152]{1,0:T(8,128)(2,1)} %param.16) | copy-start | bytes 7962628
  11.4 39.5 %all-to-all-start = ((bf16[2,1,192,3,2,576]{5,2,3,1,0,4:T(8,128)(2,1)}), bf16[2,1,192,3,2,576]{5,2,3,1,0,4:T(8,128)(2,1)}, u32[]{:S(2)}, u32[]{:S(2)}) async-start(bf16[2,1,192,3,2,576]{5,2,3,1,0,4:T(8,128)(2,1)} %copy.68), calls=%async_computation | async-start | bytes 5898240 | tf_op jit(solution)/shard_map/all_to_all | solution.py:57
  60.0 8.2 %copy-start.4 = (f32[72]{0:T(128)S(1)}, f32[72]{0:T(128)}, u32[]{:S(2)}) copy-start(f32[72]{0:T(128)} %param.17) | copy-start | bytes 868
  69.6 1.1 copy-start.1
  81.6 1.1 copy-start.1
  105.1 6.7 %copy-start.3 = (f32[2,1152]{1,0:T(2,128)S(1)}, f32[2,1152]{1,0:T(2,128)}, u32[]{:S(2)}) copy-start(f32[2,1152]{1,0:T(2,128)} %param.20) | copy-start | bytes 27652
  107.2 16.2 %all-to-all-start.1 = ((bf16[2,2,1,192,1,576]{5,3,1,4,2,0:T(8,128)(2,1)}), bf16[2,2,1,192,1,576]{5,3,1,4,2,0:T(8,128)(2,1)}, u32[]{:S(2)}, u32[]{:S(2)}) async-start(bf16[2,2,1,192,1,576]{5,3,1,4,2,0:T(8,128)(2,1)} %pad_maximum_fusion), calls=%async_computation.1 | async-start | bytes 1966080 | tf_op jit(solution)/shard_map/all_to_all | solution.py:64
  129.0 3.3 %copy-start.2 = (f32[2,1152]{1,0:T(2,128)S(1)}, f32[2,1152]{1,0:T(2,128)}, u32[]{:S(2)}) copy-start(f32[2,1152]{1,0:T(2,128)} %param.19) | copy-start | bytes 27652
  129.1 34.7 %slice-start = ((s8[7962624]{0:T(1024)(128)(4,1)}), s8[4194304]{0:T(1024)(128)(4,1)S(1)}, s32[]{:S(2)}) async-start(s8[7962624]{0:T(1024)(128)(4,1)} %bitcast.124), calls=%async_computation.4 | async-start | bytes 8388608
  132.0 31.8 %slice-start.1 = ((s8[7962624]{0:T(1024)(128)(4,1)}), s8[3768320]{0:T(1024)(128)(4,1)S(1)}, s32[]{:S(2)}) async-start(s8[7962624]{0:T(1024)(128)(4,1)} %bitcast.124), calls=%async_computation.5 | async-start | bytes 7536640
  182.7 2.3 copy-start.5
  182.8 2.3 copy-start.6
